TPU v7x, 32 devices: a whole 2x2x4 slice. The times are simulated.
32 devices in a mesh: depth: 16 (over z, y, core), filt: 2 (over x).
Axes of the slice: x: 2, y: 2, z: 4, core: 2. Of those that a mesh axis runs over, the one named last changes fastest.
Arguments:
- volume: bfloat16 [128, 16, 1024], P('filt', 'depth'), may hold values from -6 to 6
- up_weight: bfloat16 [128, 4096], P(None, 'filt'), may hold values from -0.1875 to 0.1875
- up_bias: float32 [64], P('filt'), may hold values from -3 to 3
- first_weight: bfloat16 [27, 4096], replicated, may hold values from -0.15625 to 0.15625
- first_bias: float32 [64], replicated, may hold values from -3 to 3
- second_weight: bfloat16 [27, 4096], replicated, may hold values from -0.15625 to 0.15625
- second_bias: float32 [64], replicated, may hold values from -3 to 3
Outputs:
- decoded: bfloat16 [64, 32, 32, 128], P('filt', 'depth')
All inputs are finite; a program needn't handle non-finite values.
Results may differ from a plain program's by a relative error of at most 0.0052.
Values may be sent and summed in bfloat16 or wider, within the bound.
A program may use at most 64 MiB of HBM per device.

v0:
```python
import functools

import jax
import jax.numpy as jnp
from jax import lax
from jax.experimental import pallas as pl
from jax.experimental.pallas import tpu as pltpu
from jax.sharding import PartitionSpec as P

BF = jnp.bfloat16
F32 = jnp.float32
MESH = pl.DeviceIdType.MESH


def shift_add(low, mid, high, lane):
    left = jnp.where(lane > 0, pltpu.roll(low, 1, 1), 0.0)
    right = jnp.where(lane < 127, pltpu.roll(high, 127, 1), 0.0)
    return mid + left + right


def conv_rows(src, weight, bias, plane, row, count, lane):
    parts = []
    for kd in range(3):
        for kh in range(3):
            rows = [src[plane + kd, row + kh + r] for r in range(count)]
            parts.append(jnp.concatenate(rows, axis=1))
    stacked = jnp.concatenate(parts, axis=0)
    total = jnp.dot(weight, stacked, preferred_element_type=F32)
    outs = []
    for r in range(count):
        cols = slice(128 * r, 128 * r + 128)
        value = shift_add(total[0:64, cols], total[64:128, cols], total[128:192, cols], lane)
        value = value + bias
        outs.append(jnp.maximum(value, 0.2 * value))
    return outs


def kernel(devices, vol, wt, w1, w2, bu, b1, b2, out,
           grid_in, moved, wup, ups, hid, result,
           send, recv, xsend, wsend, wrecv, osend, orecv, lsem):
    d = lax.axis_index("depth")
    f = lax.axis_index("filt")
    g = 1 - f
    core = lax.rem(d, 2)
    s = 1 - 2 * core

    def exists(t):
        return jnp.logical_and(t >= 0, t < devices)

    barrier = pltpu.get_barrier_semaphore()
    pl.semaphore_signal(barrier, inc=1, device_id=(d, g), device_id_type=MESH)
    for off in (-2, -1, 1, 2):
        @pl.when(exists(d + off))
        def _():
            pl.semaphore_signal(barrier, inc=1, device_id=(d + off, f), device_id_type=MESH)
    peers = 1
    for off in (-2, -1, 1, 2):
        peers = peers + jnp.where(exists(d + off), 1, 0)
    pl.semaphore_wait(barrier, peers)

    x_copy = pltpu.make_async_remote_copy(
        src_ref=vol.at[:, pl.ds(pl.multiple_of(384 * g, 128), 640)],
        dst_ref=grid_in.at[2, f], send_sem=xsend, recv_sem=recv.at[2, f],
        device_id=(d, g), device_id_type=MESH)
    x_copy.start()
    w_half = pl.ds(8 * core, 8)
    w_copy = pltpu.make_async_remote_copy(
        src_ref=wt.at[w_half], dst_ref=wup.at[w_half, f], send_sem=wsend.at[0], recv_sem=wrecv.at[0],
        device_id=(d, g), device_id_type=MESH)
    w_copy.start()
    grid_in[2, f] = vol[:, pl.ds(pl.multiple_of(384 * f, 128), 640)]

    def to_depth(half, which, at, target):
        slot = d - target + 2 if which < 3 else 2 - 2 * s
        return pltpu.make_async_remote_copy(
            src_ref=grid_in.at[at, half], dst_ref=grid_in.at[slot, half],
            send_sem=send.at[which, half], recv_sem=recv.at[slot, half],
            device_id=(target, f), device_id_type=MESH)

    def arrived(slot, half):
        pltpu.make_async_copy(grid_in.at[slot, half], grid_in.at[slot, half], recv.at[slot, half]).wait()

    def start_half(half):
        for which, off in enumerate((-s, s, 2 * s)):
            @pl.when(exists(d + off))
            def _():
                to_depth(half, which, 2, d + off).start()

    start_half(f)
    for off in (-2, -1, 1, 2):
        @pl.when(jnp.logical_not(exists(d + off)))
        def _():
            grid_in[2 + off] = jnp.zeros(grid_in.shape[1:], BF)
    for k in range(16):
        wup[k, f] = wt[k]
    ups[:, 0] = jnp.zeros((6, 64, 128), BF)
    ups[:, 21] = jnp.zeros((6, 64, 128), BF)
    hid[:, 0] = jnp.zeros((4, 64, 128), BF)
    hid[:, 19] = jnp.zeros((4, 64, 128), BF)

    x_recv = pltpu.make_async_copy(grid_in.at[2, g], grid_in.at[2, g], recv.at[2, g])
    x_recv.wait()
    start_half(g)

    def forward(half):
        @pl.when(exists(d - s))
        def _():
            arrived(2 - s, half)
            to_depth(half, 3, 2 - s, d + s).start()

    forward(f)
    w_other = pl.ds(8 * (1 - core), 8)
    w_copy.wait_recv()
    w_forward = pltpu.make_async_remote_copy(
        src_ref=wup.at[w_half, g], dst_ref=wup.at[w_half, g], send_sem=wsend.at[1], recv_sem=wrecv.at[1],
        device_id=(d + s, f), device_id_type=MESH)
    w_forward.start()
    forward(g)
    for half in range(2):
        arrived(2 + s, half)
    w_forward.wait_recv()

    lane = lax.broadcasted_iota(jnp.int32, (64, 128), 1)
    lane_in = lax.broadcasted_iota(jnp.int32, (128, 128), 1)
    row_at = lax.broadcasted_iota(jnp.int32, (256, 256), 0)
    col_at = lax.broadcasted_iota(jnp.int32, (256, 256), 1)
    odd, rest = row_at // 128, row_at % 128
    place = jnp.where(col_at == 128 * (rest // 64) + 2 * (rest % 64) + odd, 1.0, 0.0).astype(BF)
    bias_up, bias_1, bias_2 = bu[...], b1[...], b2[...]

    def shifted(slot):
        whole = grid_in[slot].reshape(128, 640).astype(F32)
        zero = jnp.zeros((128, 128), F32)
        turned = [zero] + [pltpu.roll(whole[:, 128 * t:128 * t + 128], 64, 1) for t in range(5)] + [zero]
        for t in range(6):
            moved[slot, :, 128 * t:128 * t + 128] = jnp.where(lane_in < 64, turned[t], turned[t + 1]).astype(BF)

    def upsample_plane(p):
        q, pd = p // 2, p % 2
        inside = exists(d - 1 + q)
        slots = (q + 1, q + 2 * pd)
        kds = (1 + pd, 3 - 3 * pd)
        for ph in range(2):
            khs = (1 + ph, 3 - 3 * ph)
            left, right = [], []
            for slot, kd in zip(slots, kds):
                for at, kh in enumerate(khs):
                    left.append(wup[4 * kd + kh].reshape(256, 128))
                    if at == 0:
                        right.append(grid_in[slot].reshape(128, 640))
                    else:
                        right.append(moved[slot, :, 128 * ph:128 * ph + 640])
            total = jnp.dot(jnp.concatenate(left, axis=1), jnp.concatenate(right, axis=0),
                            preferred_element_type=F32)
            rows = []
            for t in range(5):
                cols = slice(128 * t, 128 * t + 128)
                tap = [jnp.concatenate([total[32 * k:32 * k + 32, cols], total[128 + 32 * k:160 + 32 * k, cols]], axis=0)
                       for k in range(4)]
                even = tap[1] + jnp.where(lane % 64 > 0, pltpu.roll(tap[3], 1, 1), 0.0) + bias_up
                odd_ = tap[2] + jnp.where(lane % 64 < 63, pltpu.roll(tap[0], 127, 1), 0.0) + bias_up
                rows.append(jnp.concatenate([even, odd_], axis=1))
            both = jnp.where(inside, jnp.concatenate(rows, axis=0), 0.0).astype(BF)
            mixed = jnp.dot(both, place, preferred_element_type=F32).astype(BF)
            for t in range(5):
                for r in range(2):
                    ups[p, 1 + 2 * (2 * t + r) + ph] = mixed[64 * t:64 * t + 64, 128 * r:128 * r + 128]

    for slot in (1, 2, 3):
        shifted(slot)
    lax.fori_loop(1, 5, lambda p, c: (upsample_plane(p), c)[1], 0)

    for half in range(2):
        @pl.when(exists(d - 2 * s))
        def _():
            arrived(2 - 2 * s, half)

        @pl.when(exists(d + 2 * s))
        def _():
            arrived(2 + 2 * s, half)
    for slot in (0, 4):
        shifted(slot)
    lax.fori_loop(0, 2, lambda i, c: (upsample_plane(5 * i), c)[1], 0)

    first, second = w1[...], w2[...]

    def hidden_step(i, c):
        plane, row = i // 3, 6 * (i % 3)
        at = 2 * d - 1 + plane
        inside = jnp.logical_and(at >= 0, at < 2 * devices)
        for r, value in enumerate(conv_rows(ups, first, bias_1, plane, 2 * f + row, 6, lane)):
            hid[plane, 1 + row + r] = jnp.where(inside, value, 0.0).astype(BF)
        return c

    lax.fori_loop(0, 12, hidden_step, 0)

    rows_mine = pl.ds(16 * f, 16)

    def out_copy(plane):
        return pltpu.make_async_remote_copy(
            src_ref=result.at[plane, g], dst_ref=out.at[plane, rows_mine],
            send_sem=osend.at[plane], recv_sem=orecv.at[plane], device_id=(d, g), device_id_type=MESH)

    def own_copy(plane):
        return pltpu.make_async_copy(result.at[plane, f], out.at[plane, rows_mine], lsem.at[plane])

    for plane in range(2):
        def step(i, c):
            row = 4 * i
            for r, value in enumerate(conv_rows(hid, second, bias_2, plane, 2 * f + row, 4, lane)):
                value = value.astype(BF)
                result[plane, 0, row + r] = value[0:32]
                result[plane, 1, row + r] = value[32:64]
            return c

        lax.fori_loop(0, 4, step, 0)
        out_copy(plane).start()
        own_copy(plane).start()

    x_copy.wait_send()
    w_copy.wait_send()
    w_forward.wait_send()
    for half in range(2):
        for which, off in enumerate((-s, s, 2 * s)):
            @pl.when(exists(d + off))
            def _():
                to_depth(half, which, 2, d + off).wait_send()

        @pl.when(exists(d - s))
        def _():
            to_depth(half, 3, 2 - s, d + s).wait_send()
    for plane in range(2):
        own_copy(plane).wait()
        out_copy(plane).wait()


def shards(devices, volume, up_weight, up_bias, first_weight, first_bias, second_weight, second_bias):
    vol = volume.reshape(64, 1024)
    wt = jnp.transpose(up_weight.reshape(128, 32, 16, 4), (2, 3, 1, 0)).reshape(16, 128, 128)
    bias_up = lax.all_gather(up_bias, "filt", axis=0, tiled=True)

    def taps(weight):
        return jnp.transpose(weight.reshape(9, 3, 64, 64), (1, 2, 0, 3)).reshape(192, 576)

    vmem = pl.BlockSpec(memory_space=pltpu.VMEM)
    out = pl.pallas_call(
        functools.partial(kernel, devices),
        out_shape=jax.ShapeDtypeStruct((2, 32, 32, 128), BF),
        in_specs=[vmem] * 7,
        out_specs=vmem,
        scratch_shapes=[
            pltpu.VMEM((5, 2, 64, 640), BF),
            pltpu.VMEM((5, 128, 768), BF),
            pltpu.VMEM((16, 2, 128, 128), BF),
            pltpu.VMEM((6, 22, 64, 128), BF),
            pltpu.VMEM((4, 20, 64, 128), BF),
            pltpu.VMEM((2, 2, 16, 32, 128), BF),
            pltpu.SemaphoreType.DMA((4, 2)),
            pltpu.SemaphoreType.DMA((5, 2)),
            pltpu.SemaphoreType.DMA,
            pltpu.SemaphoreType.DMA((2,)),
            pltpu.SemaphoreType.DMA((2,)),
            pltpu.SemaphoreType.DMA((2,)),
            pltpu.SemaphoreType.DMA((2,)),
            pltpu.SemaphoreType.DMA((2,)),
        ],
        compiler_params=pltpu.CompilerParams(
            collective_id=0, has_side_effects=True, vmem_limit_bytes=48 * 1024 * 1024),
    )(vol, wt, taps(first_weight), taps(second_weight), bias_up[:, None], first_bias[:, None], second_bias[:, None])
    return jnp.transpose(out, (2, 0, 1, 3))


def solution(mesh):
    placed = (P("filt", "depth", None), P(None, "filt"), P("filt"), P(), P(), P(), P())
    return jax.shard_map(
        functools.partial(shards, mesh.shape["depth"]),
        mesh=mesh,
        in_specs=placed,
        out_specs=P("filt", "depth", None, None),
        check_vma=False,
    )
```

profile of v0, /device:TPU:0, one launch (start us, length us, event | category | flops | bytes accessed | tf_op | source)
XLA Modules:
  0.0 53.0 jit_solution(1968425915977719579)
XLA Ops:
  0.0 0.0 copy-start.6
  0.0 0.7 %copy-done.6 = u32[32]{0:T(128)S(1)} copy-done((u32[32]{0:T(128)S(1)}, u32[32]{0:T(128)}, u32[]{:S(2)}) %copy-start.6) | copy-done | bytes 152
  0.7 0.6 %dynamic-slice = u32[1]{0:T(128)} dynamic-slice(u32[32]{0:T(128)S(1)} %copy-done.6, u32[]{:T(128)S(6)} %add), dynamic_slice_sizes={1} | dynamic-slice | bytes 12
  1.9 0.0 copy-start.5
  1.9 0.6 %copy-done.5 = f32[32]{0:T(128)S(1)} copy-done((f32[32]{0:T(128)S(1)}, f32[32]{0:T(128)}, u32[]{:S(2)}) %copy-start.5) | copy-done | bytes 152
  2.5 0.2 dynamic-update-slice
  2.7 5.8 %all-reduce = f32[64]{0:T(128)S(1)} all-reduce(f32[64]{0:T(128)S(1)} %dynamic-update-slice), channel_id=1, replica_groups=mesh['depth'=16,'filt'=2] {'filt'}, use_global_device_ids=true, to_apply=%add | all-reduce | flops 64 | bytes 512
  8.5 0.0 copy-start.3
  8.6 0.1 copy.21.bu
  8.6 0.6 %copy-done.3 = f32[64]{0:T(128)S(1)} copy-done((f32[64]{0:T(128)S(1)}, f32[64]{0:T(128)}, u32[]{:S(2)}) %copy-start.3) | copy-done | bytes 280
  9.2 0.0 copy-start.4
  9.2 0.1 copy.22.b1
  9.3 0.6 %copy-done.4 = f32[64]{0:T(128)S(1)} copy-done((f32[64]{0:T(128)S(1)}, f32[64]{0:T(128)}, u32[]{:S(2)}) %copy-start.4) | copy-done | bytes 280
  9.9 0.1 copy.23.b2
  10.0 1.4 %reshape.24 = bf16[9,3,64,64]{3,2,1,0:T(8,128)(2,1)S(1)} reshape(bf16[27,4096]{1,0:T(8,128)(2,1)} %param.10) | data formatting | bytes 442368 | tf_op jit(solution)/shard_map/reshape | solution.py:243
  11.4 1.2 %copy.17 = bf16[9,3,64,64]{2,1,3,0:T(4,128)(2,1)S(1)} copy(bf16[9,3,64,64]{3,2,1,0:T(8,128)(2,1)S(1)} %reshape.24) | data formatting | bytes 442368 | tf_op jit(solution)/shard_map/reshape | solution.py:243
  12.6 0.4 reshape.25
  13.0 0.0 copy-start.2
  13.0 0.2 copy.19.w1
  13.2 0.8 %copy-done.2 = bf16[27,4096]{1,0:T(8,128)(2,1)S(1)} copy-done((bf16[27,4096]{1,0:T(8,128)(2,1)S(1)}, bf16[27,4096]{1,0:T(8,128)(2,1)}, u32[]{:S(2)}) %copy-start.2) | copy-done | bytes 221208
  13.9 0.4 reshape.26
  14.4 1.2 %copy.18 = bf16[9,3,64,64]{2,1,3,0:T(4,128)(2,1)S(1)} copy(bf16[9,3,64,64]{3,2,1,0:T(8,128)(2,1)S(1)} %reshape.26) | data formatting | bytes 442368 | tf_op jit(solution)/shard_map/reshape | solution.py:243
  15.6 0.0 copy-start.1
  15.6 0.4 reshape.27
  16.0 0.2 copy.20.w2
  16.2 0.5 copy-done.1
  16.7 0.3 copy.15
  16.9 0.0 copy-start
  16.9 0.3 copy.16
  17.3 0.5 %copy-done = bf16[64,1,1024]{2,0,1:T(8,128)(2,1)S(1)} copy-done((bf16[64,1,1024]{2,0,1:T(8,128)(2,1)S(1)}, bf16[64,1,1024]{2,0,1:T(8,128)(2,1)}, u32[]{:S(2)}) %copy-start) | copy-done | bytes 131096
  17.8 34.1 %shard_map.73 = bf16[2,32,32,128]{3,2,1,0:T(8,128)(2,1)S(1)} custom-call(bf16[64,1024]{1,0:T(8,128)(2,1)S(1)} %bitcast.18, bf16[16,128,128]{2,1,0:T(8,128)(2,1)S(1)} %bitcast.16, bf16[192,576]{1,0:T(8,128)(2,1)S(1)} %copy.19.w1, bf16[192,576]{1,0:T(8,128)(2,1)S(1)} %copy.20.w2, f32[64,1]{1,0:T(8,128)S(1)} %copy.21.bu, f32[64,1]{1,0:T(8,128)S(1)} %copy.22.b1, ...), custom_call_target="tpu_custom_call" | custom-call | tf_op jit(solution)/shard_map/pallas_call | solution.py:246
  52.0 1.0 %copy.24 = bf16[32,2,32,128]{3,2,1,0:T(8,128)(2,1)} copy(bf16[32,2,32,128]{3,0,2,1:T(8,128)(2,1)S(1)} %bitcast.17) | data formatting | bytes 1048576 | tf_op jit(solution)/shard_map/transpose | solution.py:270
  (1 shorter events, 0.0 us)
Async XLA Ops:
  0.0 0.7 %copy-start.6 = (u32[32]{0:T(128)S(1)}, u32[32]{0:T(128)}, u32[]{:S(2)}) copy-start(u32[32]{0:T(128)} %constant.3) | copy-start | bytes 388
  1.9 0.7 %copy-start.5 = (f32[32]{0:T(128)S(1)}, f32[32]{0:T(128)}, u32[]{:S(2)}) copy-start(f32[32]{0:T(128)} %param.9) | copy-start | bytes 388
  8.5 0.7 %copy-start.3 = (f32[64]{0:T(128)S(1)}, f32[64]{0:T(128)}, u32[]{:S(2)}) copy-start(f32[64]{0:T(128)} %param.11) | copy-start | bytes 772
  9.2 0.7 %copy-start.4 = (f32[64]{0:T(128)S(1)}, f32[64]{0:T(128)}, u32[]{:S(2)}) copy-start(f32[64]{0:T(128)} %param.13) | copy-start | bytes 772
  13.0 1.0 %copy-start.2 = (bf16[27,4096]{1,0:T(8,128)(2,1)S(1)}, bf16[27,4096]{1,0:T(8,128)(2,1)}, u32[]{:S(2)}) copy-start(bf16[27,4096]{1,0:T(8,128)(2,1)} %param.12) | copy-start | bytes 663556
  15.6 1.0 %copy-start.1 = (bf16[128,2048]{1,0:T(8,128)(2,1)S(1)}, bf16[128,2048]{1,0:T(8,128)(2,1)}, u32[]{:S(2)}) copy-start(bf16[128,2048]{1,0:T(8,128)(2,1)} %param.8) | copy-start | bytes 1572868
  16.9 0.9 %copy-start = (bf16[64,1,1024]{2,0,1:T(8,128)(2,1)S(1)}, bf16[64,1,1024]{2,0,1:T(8,128)(2,1)}, u32[]{:S(2)}) copy-start(bf16[64,1,1024]{2,0,1:T(8,128)(2,1)} %param.7) | copy-start | bytes 393220
where the time goes:
time: 53.3 us; the launch traced here: 53 us
  Pallas kernels  34.1 us (64%)
  local copies, waits for them, and re-layouts  12.3 us (23%)
  blocking collectives  5.81 us (11%)
  between operations  0.76 us (1%)
    pallas_call x1, Pallas kernels, shards(): pl.pallas_call(functools.partial(kernel, devices), out_shape=jax.ShapeDty...  34.1 us
    unnamed x1, blocking collectives  5.81 us
    unnamed x18, local copies, waits for them, and re-layouts  5.27 us
    reshape x4, local copies, waits for them, and re-layouts, taps(): weight.reshape(9, 3, 64, 64)  4.31 us

commit v1 on v0

--- a/solution.py
+++ b/solution.py
@@ -36,8 +36,8 @@
 
 
 def kernel(devices, vol, wt, w1, w2, bu, b1, b2, out,
-           grid_in, moved, wup, ups, hid, result,
-           send, recv, xsend, wsend, wrecv, osend, orecv, lsem):
+           grid_in, moved, wup, ups, hid, result, bmine, bother, spread, packed, wconv,
+           send, recv, xsend, wsend, wrecv, osend, orecv, lsem, bsem):
     d = lax.axis_index("depth")
     f = lax.axis_index("filt")
     g = 1 - f
@@ -68,6 +68,12 @@
         src_ref=wt.at[w_half], dst_ref=wup.at[w_half, f], send_sem=wsend.at[0], recv_sem=wrecv.at[0],
         device_id=(d, g), device_id_type=MESH)
     w_copy.start()
+    bmine[...] = jnp.zeros((8, 128), F32)
+    bmine[0:1, 0:32] = bu[...]
+    b_copy = pltpu.make_async_remote_copy(
+        src_ref=bmine, dst_ref=bother, send_sem=bsem.at[0], recv_sem=bsem.at[1],
+        device_id=(d, g), device_id_type=MESH)
+    b_copy.start()
     grid_in[2, f] = vol[:, pl.ds(pl.multiple_of(384 * f, 128), 640)]
 
     def to_depth(half, which, at, target):
@@ -80,13 +86,15 @@
     def arrived(slot, half):
         pltpu.make_async_copy(grid_in.at[slot, half], grid_in.at[slot, half], recv.at[slot, half]).wait()
 
-    def start_half(half):
-        for which, off in enumerate((-s, s, 2 * s)):
+    def start_half(half, some):
+        for which in some:
+            off = (-s, s, 2 * s)[which]
+
             @pl.when(exists(d + off))
             def _():
                 to_depth(half, which, 2, d + off).start()
 
-    start_half(f)
+    start_half(f, (0, 1))
     for off in (-2, -1, 1, 2):
         @pl.when(jnp.logical_not(exists(d + off)))
         def _():
@@ -100,7 +108,28 @@
 
     x_recv = pltpu.make_async_copy(grid_in.at[2, g], grid_in.at[2, g], recv.at[2, g])
     x_recv.wait()
-    start_half(g)
+    start_half(g, (0, 1))
+    start_half(f, (2,))
+    start_half(g, (2,))
+
+    lane_q = lax.broadcasted_iota(jnp.int32, (32, 128), 1)
+    for at, raw in enumerate((w1, w2)):
+        for q in range(32):
+            spread[32 * q:32 * q + 27, :] = raw[:, 128 * q:128 * q + 128].astype(F32)
+
+        def tap_rows(e):
+            return spread[pl.ds(e, 32, stride=32), :]
+
+        for kw in range(3):
+            for m in range(5):
+                here = tap_rows(6 * m + kw)
+                after = tap_rows(6 * m + 3 + kw) if m < 4 else jnp.zeros((32, 128), F32)
+                packed[m, pl.ds(64 * kw, 32, stride=2), :] = jnp.where(
+                    lane_q < 64, here, pltpu.roll(after, 64, 1))
+                packed[m, pl.ds(64 * kw + 1, 32, stride=2), :] = jnp.where(
+                    lane_q < 64, pltpu.roll(here, 64, 1), after)
+        for m in range(5):
+            wconv[at, :, 128 * m:128 * m + 128] = packed[m].astype(BF)
 
     def forward(half):
         @pl.when(exists(d - s))
@@ -126,7 +155,16 @@
     col_at = lax.broadcasted_iota(jnp.int32, (256, 256), 1)
     odd, rest = row_at // 128, row_at % 128
     place = jnp.where(col_at == 128 * (rest // 64) + 2 * (rest % 64) + odd, 1.0, 0.0).astype(BF)
-    bias_up, bias_1, bias_2 = bu[...], b1[...], b2[...]
+
+    def column(row, count):
+        at = lax.broadcasted_iota(jnp.int32, (count, count), 0)
+        to = lax.broadcasted_iota(jnp.int32, (count, count), 1)
+        return jnp.sum(jnp.where(at == to, row, 0.0), axis=1, keepdims=True)
+
+    b_copy.wait_recv()
+    mine, other = column(bmine[0:1, 0:32], 32), column(bother[0:1, 0:32], 32)
+    bias_up = jnp.concatenate([jnp.where(f == 0, mine, other), jnp.where(f == 0, other, mine)], axis=0)
+    bias_1, bias_2 = column(b1[...], 64), column(b2[...], 64)
 
     def shifted(slot):
         whole = grid_in[slot].reshape(128, 640).astype(F32)
@@ -170,19 +208,7 @@
         shifted(slot)
     lax.fori_loop(1, 5, lambda p, c: (upsample_plane(p), c)[1], 0)
 
-    for half in range(2):
-        @pl.when(exists(d - 2 * s))
-        def _():
-            arrived(2 - 2 * s, half)
-
-        @pl.when(exists(d + 2 * s))
-        def _():
-            arrived(2 + 2 * s, half)
-    for slot in (0, 4):
-        shifted(slot)
-    lax.fori_loop(0, 2, lambda i, c: (upsample_plane(5 * i), c)[1], 0)
-
-    first, second = w1[...], w2[...]
+    first, second = wconv[0, :, 0:576], wconv[1, :, 0:576]
 
     def hidden_step(i, c):
         plane, row = i // 3, 6 * (i % 3)
@@ -192,7 +218,20 @@
             hid[plane, 1 + row + r] = jnp.where(inside, value, 0.0).astype(BF)
         return c
 
-    lax.fori_loop(0, 12, hidden_step, 0)
+    lax.fori_loop(3, 9, hidden_step, 0)
+
+    for half in range(2):
+        @pl.when(exists(d - 2 * s))
+        def _():
+            arrived(2 - 2 * s, half)
+
+        @pl.when(exists(d + 2 * s))
+        def _():
+            arrived(2 + 2 * s, half)
+    for slot in (0, 4):
+        shifted(slot)
+    lax.fori_loop(0, 2, lambda i, c: (upsample_plane(5 * i), c)[1], 0)
+    lax.fori_loop(0, 6, lambda i, c: hidden_step(i + 6 * (i // 3), c), 0)
 
     rows_mine = pl.ds(16 * f, 16)
 
@@ -217,6 +256,7 @@
         out_copy(plane).start()
         own_copy(plane).start()
 
+    b_copy.wait_send()
     x_copy.wait_send()
     w_copy.wait_send()
     w_forward.wait_send()
@@ -237,11 +277,6 @@
 def shards(devices, volume, up_weight, up_bias, first_weight, first_bias, second_weight, second_bias):
     vol = volume.reshape(64, 1024)
     wt = jnp.transpose(up_weight.reshape(128, 32, 16, 4), (2, 3, 1, 0)).reshape(16, 128, 128)
-    bias_up = lax.all_gather(up_bias, "filt", axis=0, tiled=True)
-
-    def taps(weight):
-        return jnp.transpose(weight.reshape(9, 3, 64, 64), (1, 2, 0, 3)).reshape(192, 576)
-
     vmem = pl.BlockSpec(memory_space=pltpu.VMEM)
     out = pl.pallas_call(
         functools.partial(kernel, devices),
@@ -255,6 +290,11 @@
             pltpu.VMEM((6, 22, 64, 128), BF),
             pltpu.VMEM((4, 20, 64, 128), BF),
             pltpu.VMEM((2, 2, 16, 32, 128), BF),
+            pltpu.VMEM((8, 128), F32),
+            pltpu.VMEM((8, 128), F32),
+            pltpu.VMEM((1024, 128), F32),
+            pltpu.VMEM((5, 192, 128), F32),
+            pltpu.VMEM((2, 192, 640), BF),
             pltpu.SemaphoreType.DMA((4, 2)),
             pltpu.SemaphoreType.DMA((5, 2)),
             pltpu.SemaphoreType.DMA,
@@ -263,10 +303,11 @@
             pltpu.SemaphoreType.DMA((2,)),
             pltpu.SemaphoreType.DMA((2,)),
             pltpu.SemaphoreType.DMA((2,)),
+            pltpu.SemaphoreType.DMA((2,)),
         ],
         compiler_params=pltpu.CompilerParams(
             collective_id=0, has_side_effects=True, vmem_limit_bytes=48 * 1024 * 1024),
-    )(vol, wt, taps(first_weight), taps(second_weight), bias_up[:, None], first_bias[:, None], second_bias[:, None])
+    )(vol, wt, first_weight, second_weight, up_bias[None], first_bias[None], second_bias[None])
     return jnp.transpose(out, (2, 0, 1, 3))
 
 

time: 53.3 us -> 38.7 us (0.73)
  local copies, waits for them, and re-layouts: 12.3 us -> 3.37 us
  blocking collectives: 5.81 us -> 0 us
  Pallas kernels: 34.1 us -> 35.1 us
  between operations: 0.76 us -> 0.07 us
    unnamed x1 -> x0, blocking collectives: 5.81 us -> none
    reshape x8 -> x0, local copies, waits for them, and re-layouts: 5.38 us -> none  [the longest x4 4.31 us: taps(): weight.reshape(9, 3, 64, 64)]
    unnamed x18 -> x13, local copies, waits for them, and re-layouts: 5.27 us -> 2.03 us
    pallas_call x1, Pallas kernels: 34.1 us -> 35.1 us  [shards(): pl.pallas_call(functools.partial(kernel, devices), out_shape=jax.ShapeDty...]
where the time goes in v1:
time: 38.7 us; the launch traced here: 38.5 us
  Pallas kernels  35.1 us (91%)
  local copies, waits for them, and re-layouts  3.37 us (9%)
    pallas_call x1, Pallas kernels, shards(): pl.pallas_call(functools.partial(kernel, devices), out_shape=jax.ShapeDty...  35.1 us
    unnamed x13, local copies, waits for them, and re-layouts  2.03 us
    transpose x1, local copies, waits for them, and re-layouts, shards(): return jnp.transpose(out, (2, 0, 1, 3))  1 us

profile of v1, /device:TPU:0, one launch (start us, length us, event | category | flops | bytes accessed | tf_op | source)
XLA Modules:
  0.0 38.5 jit_solution(6711996608639366966)
XLA Ops:
  0.0 1.3 %copy.10 = bf16[128,2048]{0,1:T(8,128)(2,1)S(1)} copy(bf16[128,2048]{1,0:T(8,128)(2,1)} %param.8) | data formatting | bytes 1048576 | tf_op args[1]
  1.3 0.0 copy-start
  1.3 0.0 copy-start.1
  1.3 0.0 copy-start.2
  1.4 0.3 copy.11
  1.7 0.0 copy-start.3
  1.7 0.0 copy-start.4
  1.7 0.0 copy-start.5
  1.7 0.5 %copy-done = bf16[27,4096]{1,0:T(8,128)(2,1)S(1)} copy-done((bf16[27,4096]{1,0:T(8,128)(2,1)S(1)}, bf16[27,4096]{1,0:T(8,128)(2,1)}, u32[]{:S(2)}) %copy-start) | copy-done | bytes 221208
  2.3 0.1 copy-done.1
  2.4 0.0 copy-done.2
  2.4 0.0 copy-done.3
  2.4 0.0 copy-done.4
  2.4 0.0 copy-done.5
  2.4 35.1 %shard_map.73 = bf16[2,32,32,128]{3,2,1,0:T(8,128)(2,1)S(1)} custom-call(bf16[64,1024]{1,0:T(8,128)(2,1)S(1)} %bitcast.11, bf16[16,128,128]{2,1,0:T(8,128)(2,1)S(1)} %bitcast.9, bf16[27,4096]{1,0:T(8,128)(2,1)S(1)} %copy-done, bf16[27,4096]{1,0:T(8,128)(2,1)S(1)} %copy-done.1, f32[1,32]{1,0:T(1,128)S(1)} %bitcast.12, f32[1,64]{1,0:T(1,128)S(1)} %bitcast.13, ...), custom_call_target="tpu_custom_call" | custom-call | tf_op jit(solution)/shard_map/pallas_call | solution.py:281
  37.5 1.0 %copy.12 = bf16[32,2,32,128]{3,2,1,0:T(8,128)(2,1)} copy(bf16[32,2,32,128]{3,0,2,1:T(8,128)(2,1)S(1)} %bitcast.10) | data formatting | bytes 1048576 | tf_op jit(solution)/shard_map/transpose | solution.py:311
Async XLA Ops:
  1.3 1.0 %copy-start = (bf16[27,4096]{1,0:T(8,128)(2,1)S(1)}, bf16[27,4096]{1,0:T(8,128)(2,1)}, u32[]{:S(2)}) copy-start(bf16[27,4096]{1,0:T(8,128)(2,1)} %w1.1) | copy-start | bytes 663556
  1.3 1.0 %copy-start.1 = (bf16[27,4096]{1,0:T(8,128)(2,1)S(1)}, bf16[27,4096]{1,0:T(8,128)(2,1)}, u32[]{:S(2)}) copy-start(bf16[27,4096]{1,0:T(8,128)(2,1)} %w2.1) | copy-start | bytes 663556
  1.3 1.0 %copy-start.2 = (bf16[64,1,1024]{2,0,1:T(8,128)(2,1)S(1)}, bf16[64,1,1024]{2,0,1:T(8,128)(2,1)}, u32[]{:S(2)}) copy-start(bf16[64,1,1024]{2,0,1:T(8,128)(2,1)} %param.7) | copy-start | bytes 393220
  1.7 0.7 %copy-start.3 = (f32[32]{0:T(128)S(1)}, f32[32]{0:T(128)}, u32[]{:S(2)}) copy-start(f32[32]{0:T(128)} %param.9) | copy-start | bytes 388
  1.7 0.7 %copy-start.4 = (f32[64]{0:T(128)S(1)}, f32[64]{0:T(128)}, u32[]{:S(2)}) copy-start(f32[64]{0:T(128)} %param.11) | copy-start | bytes 772
  1.7 0.7 %copy-start.5 = (f32[64]{0:T(128)S(1)}, f32[64]{0:T(128)}, u32[]{:S(2)}) copy-start(f32[64]{0:T(128)} %param.13) | copy-start | bytes 772

commit v2 on v1

--- a/solution.py
+++ b/solution.py
@@ -18,20 +18,20 @@
     return mid + left + right
 
 
-def conv_rows(src, weight, bias, plane, row, count, lane):
-    parts = []
-    for kd in range(3):
-        for kh in range(3):
-            rows = [src[plane + kd, row + kh + r] for r in range(count)]
-            parts.append(jnp.concatenate(rows, axis=1))
-    stacked = jnp.concatenate(parts, axis=0)
-    total = jnp.dot(weight, stacked, preferred_element_type=F32)
+def conv_rows(src, weight, bias, places, lane):
+    groups = []
+    for plane, row in places:
+        groups.append(jnp.concatenate([src[plane + kd, row + i] for kd in range(3) for i in range(4)], axis=0))
+    total = jnp.dot(weight, jnp.concatenate(groups, axis=1), preferred_element_type=F32)
     outs = []
-    for r in range(count):
-        cols = slice(128 * r, 128 * r + 128)
-        value = shift_add(total[0:64, cols], total[64:128, cols], total[128:192, cols], lane)
-        value = value + bias
-        outs.append(jnp.maximum(value, 0.2 * value))
+    for at in range(len(places)):
+        cols = slice(128 * at, 128 * at + 128)
+        for j in range(2):
+            base = 192 * j
+            value = shift_add(total[base:base + 64, cols], total[base + 64:base + 128, cols],
+                              total[base + 128:base + 192, cols], lane)
+            value = value + bias
+            outs.append(jnp.maximum(value, 0.2 * value))
     return outs
 
 
@@ -120,15 +120,22 @@
         def tap_rows(e):
             return spread[pl.ds(e, 32, stride=32), :]
 
+        nothing = jnp.zeros((32, 128), F32)
         for kw in range(3):
-            for m in range(5):
-                here = tap_rows(6 * m + kw)
-                after = tap_rows(6 * m + 3 + kw) if m < 4 else jnp.zeros((32, 128), F32)
-                packed[m, pl.ds(64 * kw, 32, stride=2), :] = jnp.where(
-                    lane_q < 64, here, pltpu.roll(after, 64, 1))
-                packed[m, pl.ds(64 * kw + 1, 32, stride=2), :] = jnp.where(
-                    lane_q < 64, pltpu.roll(here, 64, 1), after)
-        for m in range(5):
+            for kd in range(3):
+                rows_of = [tap_rows(9 * kd + 3 * kh + kw) for kh in range(3)]
+                turned = [pltpu.roll(value, 64, 1) for value in rows_of]
+                for j in range(2):
+                    for pair in range(2):
+                        m, base = 2 * kd + pair, 192 * j + 64 * kw
+                        low, high = 2 * pair - j, 2 * pair + 1 - j
+                        even = rows_of[low] if 0 <= low < 3 else nothing
+                        odd_ = turned[high] if 0 <= high < 3 else nothing
+                        packed[m, pl.ds(base, 32, stride=2), :] = jnp.where(lane_q < 64, even, odd_)
+                        even = turned[low] if 0 <= low < 3 else nothing
+                        odd_ = rows_of[high] if 0 <= high < 3 else nothing
+                        packed[m, pl.ds(base + 1, 32, stride=2), :] = jnp.where(lane_q < 64, even, odd_)
+        for m in range(6):
             wconv[at, :, 128 * m:128 * m + 128] = packed[m].astype(BF)
 
     def forward(half):
@@ -208,17 +215,26 @@
         shifted(slot)
     lax.fori_loop(1, 5, lambda p, c: (upsample_plane(p), c)[1], 0)
 
-    first, second = wconv[0, :, 0:576], wconv[1, :, 0:576]
-
-    def hidden_step(i, c):
-        plane, row = i // 3, 6 * (i % 3)
-        at = 2 * d - 1 + plane
-        inside = jnp.logical_and(at >= 0, at < 2 * devices)
-        for r, value in enumerate(conv_rows(ups, first, bias_1, plane, 2 * f + row, 6, lane)):
-            hid[plane, 1 + row + r] = jnp.where(inside, value, 0.0).astype(BF)
-        return c
-
-    lax.fori_loop(3, 9, hidden_step, 0)
+    def hidden_pass(planes):
+        def step(i, c):
+            places, spots = [], []
+            for r in range(6):
+                group = 6 * i + r
+                plane = planes[0] + (planes[1] - planes[0]) * (group // 9)
+                row = 2 * (group % 9)
+                places.append((plane, 2 * f + row))
+                spots.append((plane, row))
+            values = conv_rows(ups, wconv[0], bias_1, places, lane)
+            for r, (plane, row) in enumerate(spots):
+                at = 2 * d - 1 + plane
+                inside = jnp.logical_and(at >= 0, at < 2 * devices)
+                for j in range(2):
+                    hid[plane, 1 + row + j] = jnp.where(inside, values[2 * r + j], 0.0).astype(BF)
+            return c
+
+        lax.fori_loop(0, 3, step, 0)
+
+    hidden_pass((1, 2))
 
     for half in range(2):
         @pl.when(exists(d - 2 * s))
@@ -231,7 +247,7 @@
     for slot in (0, 4):
         shifted(slot)
     lax.fori_loop(0, 2, lambda i, c: (upsample_plane(5 * i), c)[1], 0)
-    lax.fori_loop(0, 6, lambda i, c: hidden_step(i + 6 * (i // 3), c), 0)
+    hidden_pass((0, 3))
 
     rows_mine = pl.ds(16 * f, 16)
 
@@ -245,14 +261,15 @@
 
     for plane in range(2):
         def step(i, c):
-            row = 4 * i
-            for r, value in enumerate(conv_rows(hid, second, bias_2, plane, 2 * f + row, 4, lane)):
+            row = 8 * i
+            places = [(plane, 2 * f + row + 2 * r) for r in range(4)]
+            for r, value in enumerate(conv_rows(hid, wconv[1], bias_2, places, lane)):
                 value = value.astype(BF)
                 result[plane, 0, row + r] = value[0:32]
                 result[plane, 1, row + r] = value[32:64]
             return c
 
-        lax.fori_loop(0, 4, step, 0)
+        lax.fori_loop(0, 2, step, 0)
         out_copy(plane).start()
         own_copy(plane).start()
 
@@ -293,8 +310,8 @@
             pltpu.VMEM((8, 128), F32),
             pltpu.VMEM((8, 128), F32),
             pltpu.VMEM((1024, 128), F32),
-            pltpu.VMEM((5, 192, 128), F32),
-            pltpu.VMEM((2, 192, 640), BF),
+            pltpu.VMEM((6, 384, 128), F32),
+            pltpu.VMEM((2, 384, 768), BF),
             pltpu.SemaphoreType.DMA((4, 2)),
             pltpu.SemaphoreType.DMA((5, 2)),
             pltpu.SemaphoreType.DMA,

time: 38.7 us -> 36.7 us (0.948)
  Pallas kernels: 35.1 us -> 33.1 us
    pallas_call x1, Pallas kernels: 35.1 us -> 33.1 us  [shards(): pl.pallas_call(functools.partial(kernel, devices), out_shape=jax.ShapeDty...]
where the time goes in v2:
time: 36.7 us; the launch traced here: 36.6 us
  Pallas kernels  33.1 us (90%)
  local copies, waits for them, and re-layouts  3.37 us (9%)
    pallas_call x1, Pallas kernels, shards(): pl.pallas_call(functools.partial(kernel, devices), out_shape=jax.ShapeDty...  33.1 us
    unnamed x13, local copies, waits for them, and re-layouts  2.03 us
    transpose x1, local copies, waits for them, and re-layouts, shards(): return jnp.transpose(out, (2, 0, 1, 3))  1 us

profile of v2, /device:TPU:0, one launch (start us, length us, event | category | flops | bytes accessed | tf_op | source)
XLA Modules:
  0.0 36.6 jit_solution(10827938773121638891)
XLA Ops:
  0.0 1.3 %copy.10 = bf16[128,2048]{0,1:T(8,128)(2,1)S(1)} copy(bf16[128,2048]{1,0:T(8,128)(2,1)} %param.8) | data formatting | bytes 1048576 | tf_op args[1]
  1.3 0.0 copy-start
  1.3 0.0 copy-start.1
  1.3 0.0 copy-start.2
  1.4 0.3 copy.11
  1.7 0.0 copy-start.3
  1.7 0.0 copy-start.4
  1.7 0.0 copy-start.5
  1.7 0.5 %copy-done = bf16[27,4096]{1,0:T(8,128)(2,1)S(1)} copy-done((bf16[27,4096]{1,0:T(8,128)(2,1)S(1)}, bf16[27,4096]{1,0:T(8,128)(2,1)}, u32[]{:S(2)}) %copy-start) | copy-done | bytes 221208
  2.3 0.1 copy-done.1
  2.4 0.0 copy-done.2
  2.4 0.0 copy-done.3
  2.4 0.0 copy-done.4
  2.4 0.0 copy-done.5
  2.4 33.1 %shard_map.73 = bf16[2,32,32,128]{3,2,1,0:T(8,128)(2,1)S(1)} custom-call(bf16[64,1024]{1,0:T(8,128)(2,1)S(1)} %bitcast.11, bf16[16,128,128]{2,1,0:T(8,128)(2,1)S(1)} %bitcast.9, bf16[27,4096]{1,0:T(8,128)(2,1)S(1)} %copy-done, bf16[27,4096]{1,0:T(8,128)(2,1)S(1)} %copy-done.1, f32[1,32]{1,0:T(1,128)S(1)} %bitcast.12, f32[1,64]{1,0:T(1,128)S(1)} %bitcast.13, ...), custom_call_target="tpu_custom_call" | custom-call | tf_op jit(solution)/shard_map/pallas_call | solution.py:298
  35.6 1.0 %copy.12 = bf16[32,2,32,128]{3,2,1,0:T(8,128)(2,1)} copy(bf16[32,2,32,128]{3,0,2,1:T(8,128)(2,1)S(1)} %bitcast.10) | data formatting | bytes 1048576 | tf_op jit(solution)/shard_map/transpose | solution.py:328
Async XLA Ops:
  1.3 1.0 %copy-start = (bf16[27,4096]{1,0:T(8,128)(2,1)S(1)}, bf16[27,4096]{1,0:T(8,128)(2,1)}, u32[]{:S(2)}) copy-start(bf16[27,4096]{1,0:T(8,128)(2,1)} %w1.1) | copy-start | bytes 663556
  1.3 1.0 %copy-start.1 = (bf16[27,4096]{1,0:T(8,128)(2,1)S(1)}, bf16[27,4096]{1,0:T(8,128)(2,1)}, u32[]{:S(2)}) copy-start(bf16[27,4096]{1,0:T(8,128)(2,1)} %w2.1) | copy-start | bytes 663556
  1.3 1.0 %copy-start.2 = (bf16[64,1,1024]{2,0,1:T(8,128)(2,1)S(1)}, bf16[64,1,1024]{2,0,1:T(8,128)(2,1)}, u32[]{:S(2)}) copy-start(bf16[64,1,1024]{2,0,1:T(8,128)(2,1)} %param.7) | copy-start | bytes 393220
  1.7 0.7 %copy-start.3 = (f32[32]{0:T(128)S(1)}, f32[32]{0:T(128)}, u32[]{:S(2)}) copy-start(f32[32]{0:T(128)} %param.9) | copy-start | bytes 388
  1.7 0.7 %copy-start.4 = (f32[64]{0:T(128)S(1)}, f32[64]{0:T(128)}, u32[]{:S(2)}) copy-start(f32[64]{0:T(128)} %param.11) | copy-start | bytes 772
  1.7 0.7 %copy-start.5 = (f32[64]{0:T(128)S(1)}, f32[64]{0:T(128)}, u32[]{:S(2)}) copy-start(f32[64]{0:T(128)} %param.13) | copy-start | bytes 772

commit v3 on v2

--- a/solution.py
+++ b/solution.py
@@ -106,14 +106,8 @@
     hid[:, 0] = jnp.zeros((4, 64, 128), BF)
     hid[:, 19] = jnp.zeros((4, 64, 128), BF)
 
-    x_recv = pltpu.make_async_copy(grid_in.at[2, g], grid_in.at[2, g], recv.at[2, g])
-    x_recv.wait()
-    start_half(g, (0, 1))
-    start_half(f, (2,))
-    start_half(g, (2,))
-
     lane_q = lax.broadcasted_iota(jnp.int32, (32, 128), 1)
-    for at, raw in enumerate((w1, w2)):
+    def rearrange(at, raw):
         for q in range(32):
             spread[32 * q:32 * q + 27, :] = raw[:, 128 * q:128 * q + 128].astype(F32)
 
@@ -138,6 +132,16 @@
         for m in range(6):
             wconv[at, :, 128 * m:128 * m + 128] = packed[m].astype(BF)
 
+    rearrange(0, w1)
+
+    x_recv = pltpu.make_async_copy(grid_in.at[2, g], grid_in.at[2, g], recv.at[2, g])
+    x_recv.wait()
+    start_half(g, (0, 1))
+    start_half(f, (2,))
+    start_half(g, (2,))
+
+    rearrange(1, w2)
+
     def forward(half):
         @pl.when(exists(d - s))
         def _():
@@ -145,16 +149,12 @@
             to_depth(half, 3, 2 - s, d + s).start()
 
     forward(f)
-    w_other = pl.ds(8 * (1 - core), 8)
-    w_copy.wait_recv()
+    forward(g)
+    for half in range(2):
+        arrived(2 + s, half)
     w_forward = pltpu.make_async_remote_copy(
         src_ref=wup.at[w_half, g], dst_ref=wup.at[w_half, g], send_sem=wsend.at[1], recv_sem=wrecv.at[1],
         device_id=(d + s, f), device_id_type=MESH)
-    w_forward.start()
-    forward(g)
-    for half in range(2):
-        arrived(2 + s, half)
-    w_forward.wait_recv()
 
     lane = lax.broadcasted_iota(jnp.int32, (64, 128), 1)
     lane_in = lax.broadcasted_iota(jnp.int32, (128, 128), 1)
@@ -170,7 +170,6 @@
 
     b_copy.wait_recv()
     mine, other = column(bmine[0:1, 0:32], 32), column(bother[0:1, 0:32], 32)
-    bias_up = jnp.concatenate([jnp.where(f == 0, mine, other), jnp.where(f == 0, other, mine)], axis=0)
     bias_1, bias_2 = column(b1[...], 64), column(b2[...], 64)
 
     def shifted(slot):
@@ -180,7 +179,10 @@
         for t in range(6):
             moved[slot, :, 128 * t:128 * t + 128] = jnp.where(lane_in < 64, turned[t], turned[t + 1]).astype(BF)
 
-    def upsample_plane(p):
+    lane_half = lax.broadcasted_iota(jnp.int32, (32, 128), 1) % 64
+
+    def upsample_plane(p, half, bias_up):
+        rows_at = pl.ds(pl.multiple_of(32 * half, 32), 32)
         q, pd = p // 2, p % 2
         inside = exists(d - 1 + q)
         slots = (q + 1, q + 2 * pd)
@@ -190,7 +192,7 @@
             left, right = [], []
             for slot, kd in zip(slots, kds):
                 for at, kh in enumerate(khs):
-                    left.append(wup[4 * kd + kh].reshape(256, 128))
+                    left.append(wup[4 * kd + kh, half])
                     if at == 0:
                         right.append(grid_in[slot].reshape(128, 640))
                     else:
@@ -200,20 +202,33 @@
             rows = []
             for t in range(5):
                 cols = slice(128 * t, 128 * t + 128)
-                tap = [jnp.concatenate([total[32 * k:32 * k + 32, cols], total[128 + 32 * k:160 + 32 * k, cols]], axis=0)
-                       for k in range(4)]
-                even = tap[1] + jnp.where(lane % 64 > 0, pltpu.roll(tap[3], 1, 1), 0.0) + bias_up
-                odd_ = tap[2] + jnp.where(lane % 64 < 63, pltpu.roll(tap[0], 127, 1), 0.0) + bias_up
+                tap = [total[32 * k:32 * k + 32, cols] for k in range(4)]
+                even = tap[1] + jnp.where(lane_half > 0, pltpu.roll(tap[3], 1, 1), 0.0) + bias_up
+                odd_ = tap[2] + jnp.where(lane_half < 63, pltpu.roll(tap[0], 127, 1), 0.0) + bias_up
                 rows.append(jnp.concatenate([even, odd_], axis=1))
             both = jnp.where(inside, jnp.concatenate(rows, axis=0), 0.0).astype(BF)
             mixed = jnp.dot(both, place, preferred_element_type=F32).astype(BF)
             for t in range(5):
                 for r in range(2):
-                    ups[p, 1 + 2 * (2 * t + r) + ph] = mixed[64 * t:64 * t + 64, 128 * r:128 * r + 128]
+                    ups[p, 1 + 2 * (2 * t + r) + ph, rows_at, :] = mixed[32 * t:32 * t + 32, 128 * r:128 * r + 128]
 
     for slot in (1, 2, 3):
         shifted(slot)
-    lax.fori_loop(1, 5, lambda p, c: (upsample_plane(p), c)[1], 0)
+
+    def upsample_own(p, c):
+        upsample_plane(p, f, mine)
+        return c
+
+    def upsample_other(p, c):
+        upsample_plane(p, g, other)
+        return c
+
+    lax.fori_loop(1, 3, upsample_own, 0)
+    w_copy.wait_recv()
+    w_forward.start()
+    lax.fori_loop(3, 5, upsample_own, 0)
+    w_forward.wait_recv()
+    lax.fori_loop(1, 5, upsample_other, 0)
 
     def hidden_pass(planes):
         def step(i, c):
@@ -246,32 +261,31 @@
             arrived(2 + 2 * s, half)
     for slot in (0, 4):
         shifted(slot)
-    lax.fori_loop(0, 2, lambda i, c: (upsample_plane(5 * i), c)[1], 0)
+    lax.fori_loop(0, 2, lambda i, c: upsample_other(5 * i, upsample_own(5 * i, c)), 0)
     hidden_pass((0, 3))
 
-    rows_mine = pl.ds(16 * f, 16)
-
-    def out_copy(plane):
+    def piece(k):
+        return result.at[k // 2, :, pl.ds(8 * (k % 2), 8)], out.at[k // 2, pl.ds(16 * f + 8 * (k % 2), 8)]
+
+    def out_copy(k):
+        source, target = piece(k)
         return pltpu.make_async_remote_copy(
-            src_ref=result.at[plane, g], dst_ref=out.at[plane, rows_mine],
-            send_sem=osend.at[plane], recv_sem=orecv.at[plane], device_id=(d, g), device_id_type=MESH)
-
-    def own_copy(plane):
-        return pltpu.make_async_copy(result.at[plane, f], out.at[plane, rows_mine], lsem.at[plane])
-
-    for plane in range(2):
-        def step(i, c):
-            row = 8 * i
-            places = [(plane, 2 * f + row + 2 * r) for r in range(4)]
-            for r, value in enumerate(conv_rows(hid, wconv[1], bias_2, places, lane)):
-                value = value.astype(BF)
-                result[plane, 0, row + r] = value[0:32]
-                result[plane, 1, row + r] = value[32:64]
-            return c
-
-        lax.fori_loop(0, 2, step, 0)
-        out_copy(plane).start()
-        own_copy(plane).start()
+            src_ref=source.at[g], dst_ref=target,
+            send_sem=osend.at[k], recv_sem=orecv.at[k], device_id=(d, g), device_id_type=MESH)
+
+    def own_copy(k):
+        source, target = piece(k)
+        return pltpu.make_async_copy(source.at[f], target, lsem.at[k])
+
+    for k in range(4):
+        plane, row = k // 2, 8 * (k % 2)
+        places = [(plane, 2 * f + row + 2 * r) for r in range(4)]
+        for r, value in enumerate(conv_rows(hid, wconv[1], bias_2, places, lane)):
+            value = value.astype(BF)
+            result[plane, 0, row + r] = value[0:32]
+            result[plane, 1, row + r] = value[32:64]
+        out_copy(k).start()
+        own_copy(k).start()
 
     b_copy.wait_send()
     x_copy.wait_send()
@@ -286,9 +300,9 @@
         @pl.when(exists(d - s))
         def _():
             to_depth(half, 3, 2 - s, d + s).wait_send()
-    for plane in range(2):
-        own_copy(plane).wait()
-        out_copy(plane).wait()
+    for k in range(4):
+        own_copy(k).wait()
+        out_copy(k).wait()
 
 
 def shards(devices, volume, up_weight, up_bias, first_weight, first_bias, second_weight, second_bias):
@@ -317,9 +331,9 @@
             pltpu.SemaphoreType.DMA,
             pltpu.SemaphoreType.DMA((2,)),
             pltpu.SemaphoreType.DMA((2,)),
-            pltpu.SemaphoreType.DMA((2,)),
-            pltpu.SemaphoreType.DMA((2,)),
-            pltpu.SemaphoreType.DMA((2,)),
+            pltpu.SemaphoreType.DMA((4,)),
+            pltpu.SemaphoreType.DMA((4,)),
+            pltpu.SemaphoreType.DMA((4,)),
             pltpu.SemaphoreType.DMA((2,)),
         ],
         compiler_params=pltpu.CompilerParams(

time: 36.7 us -> 38 us (1.035)
  Pallas kernels: 33.1 us -> 34.4 us
    pallas_call x1, Pallas kernels: 33.1 us -> 34.4 us  [shards(): pl.pallas_call(functools.partial(kernel, devices), out_shape=jax.ShapeDty...]
where the time goes in v3:
time: 38 us; the launch traced here: 37.8 us
  Pallas kernels  34.4 us (91%)
  local copies, waits for them, and re-layouts  3.37 us (9%)
    pallas_call x1, Pallas kernels, shards(): pl.pallas_call(functools.partial(kernel, devices), out_shape=jax.ShapeDty...  34.4 us
    unnamed x13, local copies, waits for them, and re-layouts  2.03 us
    transpose x1, local copies, waits for them, and re-layouts, shards(): return jnp.transpose(out, (2, 0, 1, 3))  1 us

profile of v3, /device:TPU:0, one launch (start us, length us, event | category | flops | bytes accessed | tf_op | source)
XLA Modules:
  0.0 37.8 jit_solution(17712264012253919028)
XLA Ops:
  0.0 1.3 %copy.10 = bf16[128,2048]{0,1:T(8,128)(2,1)S(1)} copy(bf16[128,2048]{1,0:T(8,128)(2,1)} %param.8) | data formatting | bytes 1048576 | tf_op args[1]
  1.3 0.0 copy-start
  1.3 0.0 copy-start.1
  1.3 0.0 copy-start.2
  1.4 0.3 copy.11
  1.7 0.0 copy-start.3
  1.7 0.0 copy-start.4
  1.7 0.0 copy-start.5
  1.7 0.5 %copy-done = bf16[27,4096]{1,0:T(8,128)(2,1)S(1)} copy-done((bf16[27,4096]{1,0:T(8,128)(2,1)S(1)}, bf16[27,4096]{1,0:T(8,128)(2,1)}, u32[]{:S(2)}) %copy-start) | copy-done | bytes 221208
  2.3 0.1 copy-done.1
  2.4 0.0 copy-done.2
  2.4 0.0 copy-done.3
  2.4 0.0 copy-done.4
  2.4 0.0 copy-done.5
  2.4 34.4 %shard_map.73 = bf16[2,32,32,128]{3,2,1,0:T(8,128)(2,1)S(1)} custom-call(bf16[64,1024]{1,0:T(8,128)(2,1)S(1)} %bitcast.11, bf16[16,128,128]{2,1,0:T(8,128)(2,1)S(1)} %bitcast.9, bf16[27,4096]{1,0:T(8,128)(2,1)S(1)} %copy-done, bf16[27,4096]{1,0:T(8,128)(2,1)S(1)} %copy-done.1, f32[1,32]{1,0:T(1,128)S(1)} %bitcast.12, f32[1,64]{1,0:T(1,128)S(1)} %bitcast.13, ...), custom_call_target="tpu_custom_call" | custom-call | tf_op jit(solution)/shard_map/pallas_call | solution.py:312
  36.8 1.0 %copy.12 = bf16[32,2,32,128]{3,2,1,0:T(8,128)(2,1)} copy(bf16[32,2,32,128]{3,0,2,1:T(8,128)(2,1)S(1)} %bitcast.10) | data formatting | bytes 1048576 | tf_op jit(solution)/shard_map/transpose | solution.py:342
Async XLA Ops:
  1.3 1.0 %copy-start = (bf16[27,4096]{1,0:T(8,128)(2,1)S(1)}, bf16[27,4096]{1,0:T(8,128)(2,1)}, u32[]{:S(2)}) copy-start(bf16[27,4096]{1,0:T(8,128)(2,1)} %w1.1) | copy-start | bytes 663556
  1.3 1.0 %copy-start.1 = (bf16[27,4096]{1,0:T(8,128)(2,1)S(1)}, bf16[27,4096]{1,0:T(8,128)(2,1)}, u32[]{:S(2)}) copy-start(bf16[27,4096]{1,0:T(8,128)(2,1)} %w2.1) | copy-start | bytes 663556
  1.3 1.0 %copy-start.2 = (bf16[64,1,1024]{2,0,1:T(8,128)(2,1)S(1)}, bf16[64,1,1024]{2,0,1:T(8,128)(2,1)}, u32[]{:S(2)}) copy-start(bf16[64,1,1024]{2,0,1:T(8,128)(2,1)} %param.7) | copy-start | bytes 393220
  1.7 0.7 %copy-start.3 = (f32[32]{0:T(128)S(1)}, f32[32]{0:T(128)}, u32[]{:S(2)}) copy-start(f32[32]{0:T(128)} %param.9) | copy-start | bytes 388
  1.7 0.7 %copy-start.4 = (f32[64]{0:T(128)S(1)}, f32[64]{0:T(128)}, u32[]{:S(2)}) copy-start(f32[64]{0:T(128)} %param.11) | copy-start | bytes 772
  1.7 0.7 %copy-start.5 = (f32[64]{0:T(128)S(1)}, f32[64]{0:T(128)}, u32[]{:S(2)}) copy-start(f32[64]{0:T(128)} %param.13) | copy-start | bytes 772

commit v4 on v3

--- a/solution.py
+++ b/solution.py
@@ -137,24 +137,26 @@
     x_recv = pltpu.make_async_copy(grid_in.at[2, g], grid_in.at[2, g], recv.at[2, g])
     x_recv.wait()
     start_half(g, (0, 1))
+
+    rearrange(1, w2)
+
+    def forward(half):
+        @pl.when(exists(d - s))
+        def _():
+            arrived(2 - s, half)
+            to_depth(half, 3, 2 - s, d + s).start()
+
+    forward(f)
+    forward(g)
     start_half(f, (2,))
     start_half(g, (2,))
-
-    rearrange(1, w2)
-
-    def forward(half):
-        @pl.when(exists(d - s))
-        def _():
-            arrived(2 - s, half)
-            to_depth(half, 3, 2 - s, d + s).start()
-
-    forward(f)
-    forward(g)
-    for half in range(2):
-        arrived(2 + s, half)
     w_forward = pltpu.make_async_remote_copy(
         src_ref=wup.at[w_half, g], dst_ref=wup.at[w_half, g], send_sem=wsend.at[1], recv_sem=wrecv.at[1],
         device_id=(d + s, f), device_id_type=MESH)
+    w_copy.wait_recv()
+    w_forward.start()
+    for half in range(2):
+        arrived(2 + s, half)
 
     lane = lax.broadcasted_iota(jnp.int32, (64, 128), 1)
     lane_in = lax.broadcasted_iota(jnp.int32, (128, 128), 1)
@@ -170,6 +172,7 @@
 
     b_copy.wait_recv()
     mine, other = column(bmine[0:1, 0:32], 32), column(bother[0:1, 0:32], 32)
+    bias_up = jnp.concatenate([jnp.where(f == 0, mine, other), jnp.where(f == 0, other, mine)], axis=0)
     bias_1, bias_2 = column(b1[...], 64), column(b2[...], 64)
 
     def shifted(slot):
@@ -179,10 +182,7 @@
         for t in range(6):
             moved[slot, :, 128 * t:128 * t + 128] = jnp.where(lane_in < 64, turned[t], turned[t + 1]).astype(BF)
 
-    lane_half = lax.broadcasted_iota(jnp.int32, (32, 128), 1) % 64
-
-    def upsample_plane(p, half, bias_up):
-        rows_at = pl.ds(pl.multiple_of(32 * half, 32), 32)
+    def upsample_plane(p):
         q, pd = p // 2, p % 2
         inside = exists(d - 1 + q)
         slots = (q + 1, q + 2 * pd)
@@ -192,7 +192,7 @@
             left, right = [], []
             for slot, kd in zip(slots, kds):
                 for at, kh in enumerate(khs):
-                    left.append(wup[4 * kd + kh, half])
+                    left.append(wup[4 * kd + kh].reshape(256, 128))
                     if at == 0:
                         right.append(grid_in[slot].reshape(128, 640))
                     else:
@@ -202,33 +202,21 @@
             rows = []
             for t in range(5):
                 cols = slice(128 * t, 128 * t + 128)
-                tap = [total[32 * k:32 * k + 32, cols] for k in range(4)]
-                even = tap[1] + jnp.where(lane_half > 0, pltpu.roll(tap[3], 1, 1), 0.0) + bias_up
-                odd_ = tap[2] + jnp.where(lane_half < 63, pltpu.roll(tap[0], 127, 1), 0.0) + bias_up
+                tap = [jnp.concatenate([total[32 * k:32 * k + 32, cols], total[128 + 32 * k:160 + 32 * k, cols]], axis=0)
+                       for k in range(4)]
+                even = tap[1] + jnp.where(lane % 64 > 0, pltpu.roll(tap[3], 1, 1), 0.0) + bias_up
+                odd_ = tap[2] + jnp.where(lane % 64 < 63, pltpu.roll(tap[0], 127, 1), 0.0) + bias_up
                 rows.append(jnp.concatenate([even, odd_], axis=1))
             both = jnp.where(inside, jnp.concatenate(rows, axis=0), 0.0).astype(BF)
             mixed = jnp.dot(both, place, preferred_element_type=F32).astype(BF)
             for t in range(5):
                 for r in range(2):
-                    ups[p, 1 + 2 * (2 * t + r) + ph, rows_at, :] = mixed[32 * t:32 * t + 32, 128 * r:128 * r + 128]
+                    ups[p, 1 + 2 * (2 * t + r) + ph] = mixed[64 * t:64 * t + 64, 128 * r:128 * r + 128]
 
     for slot in (1, 2, 3):
         shifted(slot)
-
-    def upsample_own(p, c):
-        upsample_plane(p, f, mine)
-        return c
-
-    def upsample_other(p, c):
-        upsample_plane(p, g, other)
-        return c
-
-    lax.fori_loop(1, 3, upsample_own, 0)
-    w_copy.wait_recv()
-    w_forward.start()
-    lax.fori_loop(3, 5, upsample_own, 0)
     w_forward.wait_recv()
-    lax.fori_loop(1, 5, upsample_other, 0)
+    lax.fori_loop(1, 5, lambda p, c: (upsample_plane(p), c)[1], 0)
 
     def hidden_pass(planes):
         def step(i, c):
@@ -261,7 +249,7 @@
             arrived(2 + 2 * s, half)
     for slot in (0, 4):
         shifted(slot)
-    lax.fori_loop(0, 2, lambda i, c: upsample_other(5 * i, upsample_own(5 * i, c)), 0)
+    lax.fori_loop(0, 2, lambda i, c: (upsample_plane(5 * i), c)[1], 0)
     hidden_pass((0, 3))
 
     def piece(k):

time: 38 us -> 35.9 us (0.945)
  Pallas kernels: 34.4 us -> 32.3 us
    pallas_call x1, Pallas kernels: 34.4 us -> 32.3 us  [shards(): pl.pallas_call(functools.partial(kernel, devices), out_shape=jax.ShapeDty...]
where the time goes in v4:
time: 35.9 us; the launch traced here: 35.7 us
  Pallas kernels  32.3 us (90%)
  local copies, waits for them, and re-layouts  3.37 us (9%)
    pallas_call x1, Pallas kernels, shards(): pl.pallas_call(functools.partial(kernel, devices), out_shape=jax.ShapeDty...  32.3 us
    unnamed x13, local copies, waits for them, and re-layouts  2.03 us
    transpose x1, local copies, waits for them, and re-layouts, shards(): return jnp.transpose(out, (2, 0, 1, 3))  1 us

profile of v4, /device:TPU:0, one launch (start us, length us, event | category | flops | bytes accessed | tf_op | source)
XLA Modules:
  0.0 35.7 jit_solution(17269111947394259824)
XLA Ops:
  0.0 1.3 %copy.10 = bf16[128,2048]{0,1:T(8,128)(2,1)S(1)} copy(bf16[128,2048]{1,0:T(8,128)(2,1)} %param.8) | data formatting | bytes 1048576 | tf_op args[1]
  1.3 0.0 copy-start
  1.3 0.0 copy-start.1
  1.3 0.0 copy-start.2
  1.4 0.3 copy.11
  1.7 0.0 copy-start.3
  1.7 0.0 copy-start.4
  1.7 0.0 copy-start.5
  1.7 0.5 %copy-done = bf16[27,4096]{1,0:T(8,128)(2,1)S(1)} copy-done((bf16[27,4096]{1,0:T(8,128)(2,1)S(1)}, bf16[27,4096]{1,0:T(8,128)(2,1)}, u32[]{:S(2)}) %copy-start) | copy-done | bytes 221208
  2.3 0.1 copy-done.1
  2.4 0.0 copy-done.2
  2.4 0.0 copy-done.3
  2.4 0.0 copy-done.4
  2.4 0.0 copy-done.5
  2.4 32.3 %shard_map.73 = bf16[2,32,32,128]{3,2,1,0:T(8,128)(2,1)S(1)} custom-call(bf16[64,1024]{1,0:T(8,128)(2,1)S(1)} %bitcast.11, bf16[16,128,128]{2,1,0:T(8,128)(2,1)S(1)} %bitcast.9, bf16[27,4096]{1,0:T(8,128)(2,1)S(1)} %copy-done, bf16[27,4096]{1,0:T(8,128)(2,1)S(1)} %copy-done.1, f32[1,32]{1,0:T(1,128)S(1)} %bitcast.12, f32[1,64]{1,0:T(1,128)S(1)} %bitcast.13, ...), custom_call_target="tpu_custom_call" | custom-call | tf_op jit(solution)/shard_map/pallas_call | solution.py:300
  34.7 1.0 %copy.12 = bf16[32,2,32,128]{3,2,1,0:T(8,128)(2,1)} copy(bf16[32,2,32,128]{3,0,2,1:T(8,128)(2,1)S(1)} %bitcast.10) | data formatting | bytes 1048576 | tf_op jit(solution)/shard_map/transpose | solution.py:330
Async XLA Ops:
  1.3 1.0 %copy-start = (bf16[27,4096]{1,0:T(8,128)(2,1)S(1)}, bf16[27,4096]{1,0:T(8,128)(2,1)}, u32[]{:S(2)}) copy-start(bf16[27,4096]{1,0:T(8,128)(2,1)} %w1.1) | copy-start | bytes 663556
  1.3 1.0 %copy-start.1 = (bf16[27,4096]{1,0:T(8,128)(2,1)S(1)}, bf16[27,4096]{1,0:T(8,128)(2,1)}, u32[]{:S(2)}) copy-start(bf16[27,4096]{1,0:T(8,128)(2,1)} %w2.1) | copy-start | bytes 663556
  1.3 1.0 %copy-start.2 = (bf16[64,1,1024]{2,0,1:T(8,128)(2,1)S(1)}, bf16[64,1,1024]{2,0,1:T(8,128)(2,1)}, u32[]{:S(2)}) copy-start(bf16[64,1,1024]{2,0,1:T(8,128)(2,1)} %param.7) | copy-start | bytes 393220
  1.7 0.7 %copy-start.3 = (f32[32]{0:T(128)S(1)}, f32[32]{0:T(128)}, u32[]{:S(2)}) copy-start(f32[32]{0:T(128)} %param.9) | copy-start | bytes 388
  1.7 0.7 %copy-start.4 = (f32[64]{0:T(128)S(1)}, f32[64]{0:T(128)}, u32[]{:S(2)}) copy-start(f32[64]{0:T(128)} %param.11) | copy-start | bytes 772
  1.7 0.7 %copy-start.5 = (f32[64]{0:T(128)S(1)}, f32[64]{0:T(128)}, u32[]{:S(2)}) copy-start(f32[64]{0:T(128)} %param.13) | copy-start | bytes 772

commit v5 on v4

--- a/solution.py
+++ b/solution.py
@@ -216,7 +216,7 @@
     for slot in (1, 2, 3):
         shifted(slot)
     w_forward.wait_recv()
-    lax.fori_loop(1, 5, lambda p, c: (upsample_plane(p), c)[1], 0)
+    lax.fori_loop(1, 5, lambda p, c: (upsample_plane(p), c)[1], 0, unroll=2)
 
     def hidden_pass(planes):
         def step(i, c):
@@ -235,7 +235,7 @@
                     hid[plane, 1 + row + j] = jnp.where(inside, values[2 * r + j], 0.0).astype(BF)
             return c
 
-        lax.fori_loop(0, 3, step, 0)
+        lax.fori_loop(0, 3, step, 0, unroll=True)
 
     hidden_pass((1, 2))
 

time: 35.9 us -> 34.1 us (0.950)
  Pallas kernels: 32.3 us -> 30.5 us
    pallas_call x1, Pallas kernels: 32.3 us -> 30.5 us  [shards(): pl.pallas_call(functools.partial(kernel, devices), out_shape=jax.ShapeDty...]
where the time goes in v5:
time: 34.1 us; the launch traced here: 33.9 us
  Pallas kernels  30.5 us (89%)
  local copies, waits for them, and re-layouts  3.37 us (10%)
    pallas_call x1, Pallas kernels, shards(): pl.pallas_call(functools.partial(kernel, devices), out_shape=jax.ShapeDty...  30.5 us
    unnamed x13, local copies, waits for them, and re-layouts  2.03 us
    transpose x1, local copies, waits for them, and re-layouts, shards(): return jnp.transpose(out, (2, 0, 1, 3))  1 us

profile of v5, /device:TPU:0, one launch (start us, length us, event | category | flops | bytes accessed | tf_op | source)
XLA Modules:
  0.0 33.9 jit_solution(17147558847172617666)
XLA Ops:
  0.0 1.3 %copy.10 = bf16[128,2048]{0,1:T(8,128)(2,1)S(1)} copy(bf16[128,2048]{1,0:T(8,128)(2,1)} %param.8) | data formatting | bytes 1048576 | tf_op args[1]
  1.3 0.0 copy-start
  1.3 0.0 copy-start.1
  1.3 0.0 copy-start.2
  1.4 0.3 %copy.11 = bf16[16,4,32,128]{3,2,1,0:T(8,128)(2,1)S(1)} copy(bf16[16,4,32,128]{3,1,0,2:T(4,128)(2,1)S(1)} %bitcast.15) | data formatting | bytes 1048576 | tf_op jit(solution)/shard_map/transpose | solution.py:298
  1.7 0.0 copy-start.3
  1.7 0.0 copy-start.4
  1.7 0.0 copy-start.5
  1.7 0.5 %copy-done = bf16[27,4096]{1,0:T(8,128)(2,1)S(1)} copy-done((bf16[27,4096]{1,0:T(8,128)(2,1)S(1)}, bf16[27,4096]{1,0:T(8,128)(2,1)}, u32[]{:S(2)}) %copy-start) | copy-done | bytes 221208
  2.3 0.1 copy-done.1
  2.4 0.0 copy-done.2
  2.4 0.0 copy-done.3
  2.4 0.0 copy-done.4
  2.4 0.0 copy-done.5
  2.4 30.5 %shard_map.73 = bf16[2,32,32,128]{3,2,1,0:T(8,128)(2,1)S(1)} custom-call(bf16[64,1024]{1,0:T(8,128)(2,1)S(1)} %bitcast.11, bf16[16,128,128]{2,1,0:T(8,128)(2,1)S(1)} %bitcast.9, bf16[27,4096]{1,0:T(8,128)(2,1)S(1)} %copy-done, bf16[27,4096]{1,0:T(8,128)(2,1)S(1)} %copy-done.1, f32[1,32]{1,0:T(1,128)S(1)} %bitcast.12, f32[1,64]{1,0:T(1,128)S(1)} %bitcast.13, ...), custom_call_target="tpu_custom_call" | custom-call | tf_op jit(solution)/shard_map/pallas_call | solution.py:300
  32.9 1.0 %copy.12 = bf16[32,2,32,128]{3,2,1,0:T(8,128)(2,1)} copy(bf16[32,2,32,128]{3,0,2,1:T(8,128)(2,1)S(1)} %bitcast.10) | data formatting | bytes 1048576 | tf_op jit(solution)/shard_map/transpose | solution.py:330
Async XLA Ops:
  1.3 1.0 %copy-start = (bf16[27,4096]{1,0:T(8,128)(2,1)S(1)}, bf16[27,4096]{1,0:T(8,128)(2,1)}, u32[]{:S(2)}) copy-start(bf16[27,4096]{1,0:T(8,128)(2,1)} %w1.1) | copy-start | bytes 663556
  1.3 1.0 %copy-start.1 = (bf16[27,4096]{1,0:T(8,128)(2,1)S(1)}, bf16[27,4096]{1,0:T(8,128)(2,1)}, u32[]{:S(2)}) copy-start(bf16[27,4096]{1,0:T(8,128)(2,1)} %w2.1) | copy-start | bytes 663556
  1.3 1.0 %copy-start.2 = (bf16[64,1,1024]{2,0,1:T(8,128)(2,1)S(1)}, bf16[64,1,1024]{2,0,1:T(8,128)(2,1)}, u32[]{:S(2)}) copy-start(bf16[64,1,1024]{2,0,1:T(8,128)(2,1)} %param.7) | copy-start | bytes 393220
  1.7 0.7 %copy-start.3 = (f32[32]{0:T(128)S(1)}, f32[32]{0:T(128)}, u32[]{:S(2)}) copy-start(f32[32]{0:T(128)} %param.9) | copy-start | bytes 388
  1.7 0.7 %copy-start.4 = (f32[64]{0:T(128)S(1)}, f32[64]{0:T(128)}, u32[]{:S(2)}) copy-start(f32[64]{0:T(128)} %param.11) | copy-start | bytes 772
  1.7 0.7 %copy-start.5 = (f32[64]{0:T(128)S(1)}, f32[64]{0:T(128)}, u32[]{:S(2)}) copy-start(f32[64]{0:T(128)} %param.13) | copy-start | bytes 772
